TPU v7x, 128 devices: a whole 4x4x4 slice. The times are simulated.
128 devices in a mesh: dp: 128 (over y, z, x, core).
Axes of the slice: x: 4, y: 4, z: 4, core: 2. Of those that a mesh axis runs over, the one named last changes fastest.
Arguments:
- images: bfloat16 [98304, 1152], P('dp'), may hold values from -0.19921875 to 0.19921875
- texts: bfloat16 [98304, 1152], P('dp'), may hold values from -0.19921875 to 0.19921875
- pair_ids: int32 [98304], P('dp'), may hold values from 0 to 191
- log_scale: float32 [1], replicated, may hold values from 1 to 2.3
- bias: float32 [1], replicated, may hold values from -6 to -2
Outputs:
- grad_images: float32 [98304, 1152], P('dp')
- grad_texts: float32 [98304, 1152], P('dp')
All inputs are finite; a program needn't handle non-finite values.
Results may differ from a plain program's by a relative error of at most 0.0042.
Values may be sent and summed in bfloat16 or wider, within the bound.
No kernel may reach another device: no remote copies, remote signals or barrier semaphores. Data moves between devices by JAX's collectives and lax.ppermute only.
A program may use at most 128 MiB of HBM per device.

v0:
```python
import functools

import jax
import jax.numpy as jnp
from jax import lax
from jax.experimental import pallas as pl
from jax.experimental.pallas import tpu as pltpu
from jax.sharding import PartitionSpec as P

AXIS = "dp"
TILE = 256
ROWS = 768
LABEL_ROWS = 16
PIECES = (352, 416)
PARTS = 4
ADD_TILE = 32
LIMIT = 16 * 1024 * 1024
W_FINISH = 20e9
W_CLOSE = 20e9
W_COPIED = 20e9
W_ADD = 20e9
LOG2E = 1.4426950408889634
ANY = pl.BlockSpec(memory_space=pl.ANY)
HBM = pl.BlockSpec(memory_space=pltpu.HBM)
VMEM = pl.BlockSpec(memory_space=pltpu.VMEM)
SMEM = pl.BlockSpec(memory_space=pltpu.SMEM)


def is_even():
    return lax.rem(lax.axis_index(AXIS), 2) == 0


class Order:
    def __init__(self):
        self.token = None

    def __call__(
        self, kernel, args, in_specs, out_shape, out_specs, scratch_shapes=(), weight=20e9, **kw
    ):
        places = {id(VMEM): pltpu.VMEM, id(HBM): pltpu.HBM}
        single = not isinstance(out_shape, list)
        out_shape = [out_shape] if single else out_shape
        out_specs = [out_specs] if single else out_specs
        args = [
            pltpu.with_memory_space_constraint(arg, places[id(spec)]) if id(spec) in places else arg
            for arg, spec in zip(args, in_specs)
        ]
        n_in, n_out, first = len(args), len(out_shape), self.token is None
        if not first:
            args = [*args, self.token]
            in_specs = [*in_specs, ANY]

        def without_tokens(*refs):
            rest = refs[len(args) :]
            kernel(*refs[:n_in], *rest[:n_out], *rest[n_out + 1 :])

        *outs, self.token = pl.pallas_call(
            without_tokens,
            out_shape=[*out_shape, pltpu.VMEM((8, 128), jnp.float32)],
            in_specs=in_specs,
            out_specs=[*out_specs, VMEM],
            scratch_shapes=scratch_shapes,
            compiler_params=pltpu.CompilerParams(vmem_limit_bytes=LIMIT),
            cost_estimate=pl.CostEstimate(flops=int(weight), bytes_accessed=0, transcendentals=0),
            **kw,
        )(*args)
        return outs[0] if single else outs


def inverse_norm(rows32):
    return 1.0 / jnp.sqrt(jnp.sum(rows32 * rows32, axis=1, keepdims=True) + 1e-06)


def unit(raw):
    rows32 = raw.astype(jnp.float32)
    return (rows32 * inverse_norm(rows32)).astype(jnp.bfloat16)


def tiles_of(size):
    return [pl.ds(start, min(TILE, size - start)) for start in range(0, size, TILE)]


def put_units(raw, out):
    for rows in tiles_of(ROWS):
        out[rows, :] = unit(raw[rows, :])


def put_labels(ids, out):
    out[ROWS:, :] = jnp.zeros((LABEL_ROWS, out.shape[1]), out.dtype)
    labels = jnp.broadcast_to(ids, (LABEL_ROWS, ROWS)).astype(jnp.float32)
    out[ROWS:, :ROWS] = labels.astype(out.dtype)


def line_of(block):
    return block[ROWS:, :].astype(jnp.float32)[:1, :ROWS]


def either(first_here, one, other):
    pl.when(first_here)(one)
    pl.when(jnp.logical_not(first_here))(other)


def part_copies(src, out, sems):
    part = ROWS // PARTS
    return [
        pltpu.make_async_copy(
            src.at[pl.ds(i * part, part)], out.at[pl.ds(i * part, part)], sems.at[i]
        )
        for i in range(PARTS)
    ]


def column_of(ids):
    lines = jnp.broadcast_to(ids, (8, ROWS)).astype(jnp.float32)
    return jnp.transpose(lines)[:, :1]


def own_kernel(
    images, texts, pair_ids, u_raw, v_raw, u, v, ids, labels, flat, flat_sem, u_sems, v_sems
):
    ids_copy = pltpu.make_async_copy(pair_ids, flat, flat_sem)
    ids_copy.start()

    def start(first, second):
        for copy in part_copies(first, u_raw, u_sems) + part_copies(second, v_raw, v_sems):
            copy.start()

    either(is_even(), lambda: start(images, texts), lambda: start(texts, images))
    ids_copy.wait()
    ids[...] = jnp.reshape(flat[...], ids.shape)
    labels[...] = column_of(ids[...])
    put_labels(ids[...], u)
    put_labels(ids[...], v)
    for copy in part_copies(images, u_raw, u_sems):
        copy.wait()
    put_units(u_raw, u)
    for copy in part_copies(texts, v_raw, v_sems):
        copy.wait()
    put_units(v_raw, v)


def own_blocks(call, images, texts, pair_ids):
    raw = pltpu.VMEM(images.shape, images.dtype)
    labelled = pltpu.VMEM((ROWS + LABEL_ROWS, images.shape[1]), images.dtype)
    return call(
        own_kernel,
        [images, texts, pair_ids],
        [HBM] * 3,
        [
            raw,
            raw,
            labelled,
            labelled,
            pltpu.VMEM((1, ROWS), pair_ids.dtype),
            pltpu.VMEM((ROWS, 1), jnp.float32),
        ],
        out_specs=[VMEM] * 6,
        scratch_shapes=[
            pltpu.VMEM(pair_ids.shape, pair_ids.dtype),
            pltpu.SemaphoreType.DMA,
            pltpu.SemaphoreType.DMA((PARTS,)),
            pltpu.SemaphoreType.DMA((PARTS,)),
        ],
        name="own_blocks",
    )


def neighbour_kernel(left_images, right_texts, ids, raw, out, labels):
    def take(src):
        for rows in tiles_of(ROWS):
            raw[rows, :] = src[rows, :]

    either(is_even(), lambda: take(left_images), lambda: take(right_texts))
    put_units(raw, out)
    put_labels(ids[...], out)
    labels[...] = column_of(ids[...])


def neighbour_block(call, left_images, right_texts, ids):
    width = left_images.shape[1]
    return call(
        neighbour_kernel,
        [left_images, right_texts, ids],
        [VMEM] * 3,
        [
            pltpu.VMEM((ROWS, width), left_images.dtype),
            pltpu.VMEM((ROWS + LABEL_ROWS, width), left_images.dtype),
            pltpu.VMEM((ROWS, 1), jnp.float32),
        ],
        out_specs=[VMEM] * 3,
        name="neighbour_block",
    )


def copy_kernel(*refs):
    half = len(refs) // 2
    for value, out in zip(refs[:half], refs[half:]):
        out[...] = value[...]


def copied(call, *values):
    return call(
        copy_kernel,
        values,
        [VMEM] * len(values),
        [pltpu.VMEM(value.shape, value.dtype) for value in values],
        out_specs=[VMEM] * len(values),
        name="copied",
        weight=W_COPIED,
    )


def contributions(log_scale, bias, labels_x, x, y, begin=0, end=ROWS):
    scale = jnp.exp(jnp.full((1, ROWS), log_scale[0], jnp.float32))
    rate = scale * -LOG2E
    shift = bias[0] * -LOG2E
    labels_y = line_of(y)
    tiles = [
        pl.ds(start, min(TILE, end - start)) for start in range(begin, end, TILE)
    ]

    def products(rows):
        return lax.dot_general(
            x[rows, :], y[:ROWS, :], (((1,), (1,)), ((), ())), preferred_element_type=jnp.float32
        )

    ahead = products(tiles[0])
    for i, rows in enumerate(tiles):
        now = ahead
        if i + 1 < len(tiles):
            ahead = products(tiles[i + 1])
        sigmoid = 1.0 / (1.0 + jnp.exp2(now * rate + shift))
        same = jnp.where(labels_x[rows, :] == labels_y, 1.0, 0.0)
        coef = ((sigmoid - same) * scale).astype(jnp.bfloat16)
        yield rows, jnp.dot(coef, y[:ROWS, :], preferred_element_type=jnp.float32)


def back_through(raw, grad):
    rows32 = raw.astype(jnp.float32)
    inverse = inverse_norm(rows32)
    exact = rows32 * inverse
    return (grad - exact * jnp.sum(exact * grad, axis=1, keepdims=True)) * inverse


def score_kernel(log_scale, bias, labels_x, x, y, *refs):
    out = refs[-1]
    for rows, grad in contributions(log_scale, bias, labels_x, x, y):
        out[rows, :] = refs[0][rows, :] + grad if len(refs) > 1 else grad


def score(call, scalars, labels_x, x, y, before=None):
    args = [*scalars, labels_x, x, y] + ([before] if before is not None else [])
    return call(
        score_kernel,
        args,
        [SMEM, SMEM] + [VMEM] * (len(args) - 2),
        pltpu.VMEM((ROWS, x.shape[1]), jnp.float32),
        out_specs=VMEM,
        input_output_aliases={5: 0} if before is not None else {},
        name="score",
    )


def close_kernel(log_scale, bias, labels_x, x, y, before, raw, out):
    for rows, grad in contributions(log_scale, bias, labels_x, x, y):
        out[rows, :] = back_through(raw[rows, :], before[rows, :] + grad)


def close(call, scalars, labels_x, x, y, before, raw):
    args = [*scalars, labels_x, x, y, before, raw]
    return call(
        close_kernel,
        args,
        [SMEM, SMEM] + [VMEM] * (len(args) - 2),
        pltpu.VMEM((ROWS, x.shape[1]), jnp.float32),
        out_specs=VMEM,
        input_output_aliases={5: 0},
        name="close",
        weight=W_CLOSE,
    )


def part_kernel(begin, log_scale, bias, labels_x, x, y, raw, *outs):
    end = begin + sum(out.shape[0] for out in outs)
    starts = [begin + sum(out.shape[0] for out in outs[:i]) for i in range(len(outs))]
    for rows, grad in contributions(log_scale, bias, labels_x, x, y, begin, end):
        result = back_through(raw[rows, :], grad).astype(outs[0].dtype)
        for out, start in zip(outs, starts):
            low, high = max(rows.start, start), min(rows.start + rows.size, start + out.shape[0])
            if low < high:
                out[low - start : high - start, :] = result[low - rows.start : high - rows.start]


def part(call, scalars, labels_x, x, y, raw, begin, sizes):
    return call(
        functools.partial(part_kernel, begin),
        [*scalars, labels_x, x, y, raw],
        [SMEM, SMEM, VMEM, VMEM, VMEM, VMEM],
        [pltpu.VMEM((size, x.shape[1]), x.dtype) for size in sizes],
        out_specs=[VMEM] * len(sizes),
        name="part",
    )


def finish_kernel(
    log_scale, bias, labels_x, x, y, before, raw, closed, image_grad, text_grad, sems
):
    copies = []
    for rows, grad in contributions(log_scale, bias, labels_x, x, y):
        closed[rows, :] = back_through(raw[rows, :], before[rows, :] + grad)
        image_copy, text_copy = [
            pltpu.make_async_copy(closed.at[rows], out.at[rows], sems.at[len(copies)])
            for out in (image_grad, text_grad)
        ]
        either(is_even(), image_copy.start, text_copy.start)
        copies.append(image_copy)
    for copy in copies:
        copy.wait()


def finish(call, scalars, labels_x, x, y, before, raw):
    shape = (ROWS, x.shape[1])
    _, *outs = call(
        finish_kernel,
        [*scalars, labels_x, x, y, before, raw],
        [SMEM, SMEM] + [VMEM] * 5,
        [pltpu.VMEM(shape, jnp.float32)] + [pltpu.HBM(shape, jnp.float32)] * 2,
        out_specs=[VMEM, HBM, HBM],
        input_output_aliases={5: 0},
        scratch_shapes=[pltpu.SemaphoreType.DMA((len(tiles_of(ROWS)),))],
        name="finish",
        weight=W_FINISH,
    )
    return outs


def add_kernel(begin, _image_grad, _text_grad, closed, piece, image_grad, text_grad, stage, sems):
    tiles = [pl.ds(start, ADD_TILE) for start in range(0, piece.shape[0], ADD_TILE)]

    def work(target):
        copies = []
        for rows in tiles:
            there = pl.ds(begin + rows.start, rows.size)
            stage[rows, :] = closed[there, :] + piece[rows, :].astype(jnp.float32)
            copies.append(
                pltpu.make_async_copy(stage.at[rows], target.at[there], sems.at[len(copies)])
            )
            copies[-1].start()
        for copy in copies:
            copy.wait()

    either(is_even(), lambda: work(text_grad), lambda: work(image_grad))


def add(call, closed, piece, outs, begin):
    size, width = piece.shape
    return call(
        functools.partial(add_kernel, begin),
        [*outs, closed, piece],
        [HBM, HBM, VMEM, VMEM],
        [pltpu.HBM((ROWS, width), jnp.float32)] * 2,
        out_specs=[HBM, HBM],
        input_output_aliases={0: 0, 1: 1},
        scratch_shapes=[
            pltpu.VMEM((size, width), jnp.float32),
            pltpu.SemaphoreType.DMA((size // ADD_TILE,)),
        ],
        name="add",
        weight=W_ADD,
    )


def pairs_of(even_step, odd_step):
    count = lax.axis_size(AXIS)
    return [(p, (p + (odd_step if p % 2 else even_step)) % count) for p in range(count)]


def permute(value, even_step, odd_step):
    return lax.ppermute(value, AXIS, pairs_of(even_step, odd_step))


def swap(value):
    return permute(value, 1, -1)


def across(value):
    return permute(value, -1, 1)


def on_device(images, texts, pair_ids, log_scale, bias):
    call = Order()
    scalars = (log_scale, bias)
    left_images = permute(images, 1, 1)
    right_texts = permute(texts, -1, -1)

    u_raw, v_raw, u, v, ids, labels = own_blocks(call, images, texts, pair_ids)
    grad_u = score(call, scalars, labels, u, v)
    grad_v = score(call, scalars, labels, v, u)
    u_again, ids_again = copied(call, u, ids)
    y = permute(u_again, 3, -3)
    s0 = swap(u_again)
    near_ids = across(ids_again)

    x_raw, x, near_labels = neighbour_block(call, left_images, right_texts, near_ids)
    s1 = swap(x)
    grad_u = score(call, scalars, labels, u, s0, grad_u)
    early, late = part(call, scalars, near_labels, x, s1, x_raw, 0, PIECES)
    early, late = across(early), across(late)
    grad_v = score(call, scalars, labels, v, x, grad_v)
    grad_u = score(call, scalars, labels, u, s1, grad_u)

    s2 = swap(*copied(call, y))
    outs = finish(call, scalars, labels, u, y, grad_u, u_raw)
    closed = close(call, scalars, labels, v, s2, grad_v, v_raw)
    outs = add(call, closed, early, outs, 0)
    return tuple(add(call, closed, late, outs, PIECES[0]))


def solution(mesh):
    in_specs = (P("dp", None), P("dp", None), P("dp"), P(), P())
    out_specs = (P("dp", None), P("dp", None))
    return jax.shard_map(
        on_device, mesh=mesh, in_specs=in_specs, out_specs=out_specs, check_vma=False
    )
```

profile of v0, /device:TPU:0, one launch (start us, length us, event | category | flops | bytes accessed | tf_op | source)
XLA Modules:
  0.0 71.0 jit_solution(9393548913762591935)
XLA Ops:
  0.6 0.1 collective-permute-start.1
  0.7 8.3 %collective-permute-start.2 = (bf16[768,1152]{1,0:T(8,128)(2,1)}, bf16[768,1152]{1,0:T(8,128)(2,1)S(1)}, u32[]{:S(2)}, u32[]{:S(2)}) collective-permute-start(bf16[768,1152]{1,0:T(8,128)(2,1)} %refs_1_.9), channel_id=1, source_target_pairs={{0,127},{1,0},{2,1},{3,2},{4,3},{5,4},{6,5},{7,6},{8,7},{9,8},{10,... | collective-permute-start | bytes 5308424 | tf_op jit(solution)/shard_map/ppermute | solution.py:379
  10.3 3.4 %own_blocks.1 = (bf16[768,1152]{1,0:T(8,128)(2,1)S(1)}, bf16[768,1152]{1,0:T(8,128)(2,1)S(1)}, bf16[784,1152]{1,0:T(8,128)(2,1)S(1)}, bf16[784,1152]{1,0:T(8,128...) custom-call(bf16[768,1152]{1,0:T(8,128)(2,1)} %refs_0_.9, ...), custom_call_target="tpu_custom_call" | custom-call | flops 20000000000 | tf_op jit(solution)/shard_map/own_blocks/pallas_call | solution.py:57
  13.7 3.4 %score.5 = (f32[768,1152]{1,0:T(8,128)S(1)}, f32[8,128]{1,0:T(8,128)S(1)}) custom-call(f32[1]{0:T(128)S(6)} %copy.25.refs_0_, f32[1]{0:T(128)S(6)} %copy.26.refs_1_, f32[768,1]{1,0:T(8,128)S(1)} %get-tuple-element.41.refs_2_, bf16[784,1152]{1,0:T(8,128)(2,1)S(1)} %get-tuple-element.42.refs_3_.refs_4_.refs_0_, ...), custom_call_target="tpu_custom_call" | custom-call | flops 20000000000 | tf_op jit(solution)/shard_map/score/pallas_call | solution.py:57
  17.1 3.5 %score.6 = (f32[768,1152]{1,0:T(8,128)S(1)}, f32[8,128]{1,0:T(8,128)S(1)}) custom-call(f32[1]{0:T(128)S(6)} %copy.25.refs_0_, f32[1]{0:T(128)S(6)} %copy.26.refs_1_, f32[768,1]{1,0:T(8,128)S(1)} %get-tuple-element.41.refs_2_, bf16[784,1152]{1,0:T(8,128)(2,1)S(1)} %get-tuple-element.44.refs_4_.refs_3_, ...), custom_call_target="tpu_custom_call" | custom-call | flops 20000000000 | tf_op jit(solution)/shard_map/score/pallas_call | solution.py:57
  20.6 0.1 copied.2
  20.7 0.7 collective-permute-start.3
  21.4 0.0 collective-permute-start.5
  21.4 0.0 collective-permute-start
  21.4 8.2 %collective-permute-done.3.refs_2_ = s32[1,768]{1,0:T(1,128)S(1)} collective-permute-done((s32[1,768]{1,0:T(1,128)S(1)}, s32[1,768]{1,0:T(1,128)S(1)}, u32[]{:S(2)}, u32[]{:S(2)}) %collective-permute-start.3) | collective-permute-done | bytes 3104 | tf_op jit(solution)/shard_map/ppermute | solution.py:379
  29.6 0.0 collective-permute-done.1.refs_0_
  29.6 0.0 collective-permute-done.2.refs_1_
  29.6 0.9 %neighbour_block.1 = (bf16[768,1152]{1,0:T(8,128)(2,1)S(1)}, bf16[784,1152]{1,0:T(8,128)(2,1)S(1)}, f32[768,1]{1,0:T(8,128)S(1)}, f32[8,128]{1,0:T(8,128)S(1)}) custom-call(bf16[768,1152]{1,0:T(8,128)(2,1)S(1)} %collective-permute-done.1.refs_0_, bf16[768,1152]{1,0:T(8,128)(2,1)S(1)} %collective-permute-done.2.refs_1_, ...), custom_call_target="tpu_custom_call" | custom-call | flops 20000000000 | tf_op jit(solution)/shard_map/neighbour_block/pallas_call | solution.py:57
  30.5 0.3 collective-permute-start.4
  30.8 0.0 collective-permute-done.5.refs_4_
  30.8 3.6 %score.7 = (f32[768,1152]{1,0:T(8,128)S(1)}, f32[8,128]{1,0:T(8,128)S(1)}) custom-call(f32[1]{0:T(128)S(6)} %copy.25.refs_0_, f32[1]{0:T(128)S(6)} %copy.26.refs_1_, f32[768,1]{1,0:T(8,128)S(1)} %get-tuple-element.41.refs_2_, bf16[784,1152]{1,0:T(8,128)(2,1)S(1)} %get-tuple-element.42.refs_3_.refs_4_.refs_0_, ...), custom_call_target="tpu_custom_call", output_to_operand_aliasing={{0}: (5, {})} | custom-call | flops 20000000000 | tf_op jit(solution)/shard_map/score/pallas_call | solution.py:57
  34.4 0.1 collective-permute-done.4.refs_4_
  34.5 4.3 %part.1 = (bf16[352,1152]{1,0:T(8,128)(2,1)S(1)}, bf16[416,1152]{1,0:T(8,128)(2,1)S(1)}, f32[8,128]{1,0:T(8,128)S(1)}) custom-call(f32[1]{0:T(128)S(6)} %copy.25.refs_0_, f32[1]{0:T(128)S(6)} %copy.26.refs_1_, f32[768,1]{1,0:T(8,128)S(1)} %get-tuple-element.56.refs_2_, bf16[784,1152]{1,0:T(8,128)(2,1)S(1)} %get-tuple-element.51.refs_3_.refs_4_, ...), custom_call_target="tpu_custom_call" | custom-call | flops 20000000000 | tf_op jit(solution)/shard_map/part/pallas_call | solution.py:57
  38.8 7.7 %collective-permute-start.7 = (bf16[352,1152]{1,0:T(8,128)(2,1)S(1)}, bf16[352,1152]{1,0:T(8,128)(2,1)S(1)}, u32[]{:S(2)}, u32[]{:S(2)}) collective-permute-start(bf16[352,1152]{1,0:T(8,128)(2,1)S(1)} %get-tuple-element.72), channel_id=1, source_target_pairs={{0,127},{1,2},{2,1},{3,4},{4,3},{5,6},{6,5},{7,8},{8,7},{9,10},{10... | collective-permute-start | bytes 2433032 | tf_op jit(solution)/shard_map/ppermute | solution.py:379
  46.5 0.3 collective-permute-start.8
  46.8 3.7 %score.8 = (f32[768,1152]{1,0:T(8,128)S(1)}, f32[8,128]{1,0:T(8,128)S(1)}) custom-call(f32[1]{0:T(128)S(6)} %copy.25.refs_0_, f32[1]{0:T(128)S(6)} %copy.26.refs_1_, f32[768,1]{1,0:T(8,128)S(1)} %get-tuple-element.41.refs_2_, bf16[784,1152]{1,0:T(8,128)(2,1)S(1)} %get-tuple-element.44.refs_4_.refs_3_, ...), custom_call_target="tpu_custom_call", output_to_operand_aliasing={{0}: (5, {})} | custom-call | flops 20000000000 | tf_op jit(solution)/shard_map/score/pallas_call | solution.py:57
  50.5 3.7 %score.9 = (f32[768,1152]{1,0:T(8,128)S(1)}, f32[8,128]{1,0:T(8,128)S(1)}) custom-call(f32[1]{0:T(128)S(6)} %copy.25.refs_0_, f32[1]{0:T(128)S(6)} %copy.26.refs_1_, f32[768,1]{1,0:T(8,128)S(1)} %get-tuple-element.41.refs_2_, bf16[784,1152]{1,0:T(8,128)(2,1)S(1)} %get-tuple-element.42.refs_3_.refs_4_.refs_0_, ...), custom_call_target="tpu_custom_call", output_to_operand_aliasing={{0}: (5, {})} | custom-call | flops 20000000000 | tf_op jit(solution)/shard_map/score/pallas_call | solution.py:57
  54.2 0.0 collective-permute-done.refs_0_.refs_4_
  54.3 0.1 copied.3
  54.4 0.3 collective-permute-start.6
  54.7 5.4 %finish.1 = (f32[768,1152]{1,0:T(8,128)S(1)}, f32[768,1152]{1,0:T(8,128)}, f32[768,1152]{1,0:T(8,128)}, f32[8,128]{1,0:T(8,128)S(1)}) custom-call(f32[1]{0:T(128)S(6)} %copy.25.refs_0_, f32[1]{0:T(128)S(6)} %copy.26.refs_1_, f32[768,1]{1,0:T(8,128)S(1)} %get-tuple-element.41.refs_2_, ...), custom_call_target="tpu_custom_call", output_to_operand_aliasing={{0}: (5, {})} | custom-call | flops 20000000000 | tf_op jit(solution)/shard_map/finish/pallas_call | solution.py:57
  60.2 0.0 collective-permute-done.6.refs_4_
  60.2 4.5 %close.1 = (f32[768,1152]{1,0:T(8,128)S(1)}, f32[8,128]{1,0:T(8,128)S(1)}) custom-call(f32[1]{0:T(128)S(6)} %copy.25.refs_0_, f32[1]{0:T(128)S(6)} %copy.26.refs_1_, f32[768,1]{1,0:T(8,128)S(1)} %get-tuple-element.41.refs_2_, bf16[784,1152]{1,0:T(8,128)(2,1)S(1)} %get-tuple-element.44.refs_4_.refs_3_, ...), custom_call_target="tpu_custom_call", output_to_operand_aliasing={{0}: (5, {})} | custom-call | flops 20000000000 | tf_op jit(solution)/shard_map/close/pallas_call | solution.py:57
  64.7 0.0 collective-permute-done.7.refs_3_
  64.7 1.3 %add.2 = (f32[768,1152]{1,0:T(8,128)}, f32[768,1152]{1,0:T(8,128)}, f32[8,128]{1,0:T(8,128)S(1)}) custom-call(f32[768,1152]{1,0:T(8,128)} %get-tuple-element.65.refs_0_, f32[768,1152]{1,0:T(8,128)} %get-tuple-element.66.refs_1_, f32[768,1152]{1,0:T(8,128)S(1)} %get-tuple-element.71.refs_2_, ...), custom_call_target="tpu_custom_call", output_to_operand_aliasing={{0}: (0, {}), {1}: (1, {})} | custom-call | flops 20000000000 | tf_op jit(solution)/shard_map/add/pallas_call | solution.py:57
  66.0 2.8 %collective-permute-done.8.refs_3_ = bf16[416,1152]{1,0:T(8,128)(2,1)S(1)} collective-permute-done((bf16[416,1152]{1,0:T(8,128)(2,1)S(1)}, bf16[416,1152]{1,0:T(8,128)(2,1)S(1)}, u32[]{:S(2)}, u32[]{:S(2)}) %collective-permute-start.8) | collective-permute-done | bytes 958496 | tf_op jit(solution)/shard_map/ppermute | solution.py:379
  68.8 2.0 %add.3 = (f32[768,1152]{1,0:T(8,128)}, f32[768,1152]{1,0:T(8,128)}, f32[8,128]{1,0:T(8,128)}) custom-call(f32[768,1152]{1,0:T(8,128)} %get-tuple-element.74.refs_0_, f32[768,1152]{1,0:T(8,128)} %get-tuple-element.75.refs_1_, f32[768,1152]{1,0:T(8,128)S(1)} %get-tuple-element.71.refs_2_, ...), custom_call_target="tpu_custom_call", output_to_operand_aliasing={{0}: (0, {}), {1}: (1, {})} | custom-call | flops 20000000000 | tf_op jit(solution)/shard_map/add/pallas_call | solution.py:57
Async XLA Ops:
  0.6 29.0 %collective-permute-start.1 = (bf16[768,1152]{1,0:T(8,128)(2,1)}, bf16[768,1152]{1,0:T(8,128)(2,1)S(1)}, u32[]{:S(2)}, u32[]{:S(2)}) collective-permute-start(bf16[768,1152]{1,0:T(8,128)(2,1)} %refs_0_.9), channel_id=1, source_target_pairs={{0,1},{1,2},{2,3},{3,4},{4,5},{5,6},{6,7},{7,8},{8,9},{9,10},{10,1... | collective-permute-start | bytes 5308424 | tf_op jit(solution)/shard_map/ppermute | solution.py:379
  0.7 28.9 %collective-permute-start.2 = (bf16[768,1152]{1,0:T(8,128)(2,1)}, bf16[768,1152]{1,0:T(8,128)(2,1)S(1)}, u32[]{:S(2)}, u32[]{:S(2)}) collective-permute-start(bf16[768,1152]{1,0:T(8,128)(2,1)} %refs_1_.9), channel_id=1, source_target_pairs={{0,127},{1,0},{2,1},{3,2},{4,3},{5,4},{6,5},{7,6},{8,7},{9,8},{10,... | collective-permute-start | bytes 5308424 | tf_op jit(solution)/shard_map/ppermute | solution.py:379
  20.7 8.9 %collective-permute-start.3 = (s32[1,768]{1,0:T(1,128)S(1)}, s32[1,768]{1,0:T(1,128)S(1)}, u32[]{:S(2)}, u32[]{:S(2)}) collective-permute-start(s32[1,768]{1,0:T(1,128)S(1)} %get-tuple-element.49), channel_id=1, source_target_pairs={{0,127},{1,2},{2,1},{3,4},{4,3},{5,6},{6,5},{7,8},{8,7},{9,10},{10... | collective-permute-start | bytes 9224 | tf_op jit(solution)/shard_map/ppermute | solution.py:379
  21.4 9.4 %collective-permute-start.5 = (bf16[784,1152]{1,0:T(8,128)(2,1)S(1)}, bf16[784,1152]{1,0:T(8,128)(2,1)S(1)}, u32[]{:S(2)}, u32[]{:S(2)}) collective-permute-start(bf16[784,1152]{1,0:T(8,128)(2,1)S(1)} %get-tuple-element.48), channel_id=1, source_target_pairs={{0,1},{1,0},{2,3},{3,2},{4,5},{5,4},{6,7},{7,6},{8,9},{9,8},{10,11... | collective-permute-start | bytes 5419016 | tf_op jit(solution)/shard_map/ppermute | solution.py:379
  21.4 32.8 %collective-permute-start = (bf16[784,1152]{1,0:T(8,128)(2,1)S(1)}, bf16[784,1152]{1,0:T(8,128)(2,1)S(1)}, u32[]{:S(2)}, u32[]{:S(2)}) collective-permute-start(bf16[784,1152]{1,0:T(8,128)(2,1)S(1)} %get-tuple-element.48), channel_id=1, source_target_pairs={{0,3},{1,126},{2,5},{3,0},{4,7},{5,2},{6,9},{7,4},{8,11},{9,6},{10... | collective-permute-start | bytes 5419016 | tf_op jit(solution)/shard_map/ppermute | solution.py:379
  30.5 4.0 %collective-permute-start.4 = (bf16[784,1152]{1,0:T(8,128)(2,1)S(1)}, bf16[784,1152]{1,0:T(8,128)(2,1)S(1)}, u32[]{:S(2)}, u32[]{:S(2)}) collective-permute-start(bf16[784,1152]{1,0:T(8,128)(2,1)S(1)} %get-tuple-element.51.refs_3_.refs_4_), channel_id=1, source_target_pairs={{0,1},{1,0},{2,3},{3,2},{4,5},{5,4},{6,7},{7,6},{8,9},{9,8},{10,11... | collective-permute-start | bytes 5419016 | tf_op jit(solution)/shard_map/ppermute | solution.py:379
  38.8 25.9 %collective-permute-start.7 = (bf16[352,1152]{1,0:T(8,128)(2,1)S(1)}, bf16[352,1152]{1,0:T(8,128)(2,1)S(1)}, u32[]{:S(2)}, u32[]{:S(2)}) collective-permute-start(bf16[352,1152]{1,0:T(8,128)(2,1)S(1)} %get-tuple-element.72), channel_id=1, source_target_pairs={{0,127},{1,2},{2,1},{3,4},{4,3},{5,6},{6,5},{7,8},{8,7},{9,10},{10... | collective-permute-start | bytes 2433032 | tf_op jit(solution)/shard_map/ppermute | solution.py:379
  46.5 22.3 %collective-permute-start.8 = (bf16[416,1152]{1,0:T(8,128)(2,1)S(1)}, bf16[416,1152]{1,0:T(8,128)(2,1)S(1)}, u32[]{:S(2)}, u32[]{:S(2)}) collective-permute-start(bf16[416,1152]{1,0:T(8,128)(2,1)S(1)} %get-tuple-element.76), channel_id=1, source_target_pairs={{0,127},{1,2},{2,1},{3,4},{4,3},{5,6},{6,5},{7,8},{8,7},{9,10},{10... | collective-permute-start | bytes 2875400 | tf_op jit(solution)/shard_map/ppermute | solution.py:379
  54.4 5.8 %collective-permute-start.6 = (bf16[784,1152]{1,0:T(8,128)(2,1)S(1)}, bf16[784,1152]{1,0:T(8,128)(2,1)S(1)}, u32[]{:S(2)}, u32[]{:S(2)}) collective-permute-start(bf16[784,1152]{1,0:T(8,128)(2,1)S(1)} %get-tuple-element.67), channel_id=1, source_target_pairs={{0,1},{1,0},{2,3},{3,2},{4,5},{5,4},{6,7},{7,6},{8,9},{9,8},{10,11... | collective-permute-start | bytes 5419016 | tf_op jit(solution)/shard_map/ppermute | solution.py:379
where the time goes:
time: 71.1 us; the launch traced here: 71 us
  Pallas kernels  39.9 us (56%)
  starting transfers between devices  17.6 us (25%)
  waiting for transfers between devices  11.2 us (16%)
  between operations  2.27 us (3%)
    pallas_call x14, Pallas kernels, __call__(): pl.pallas_call(without_tokens, out_shape=[*out_shape, pltpu.VMEM((8, 128)...  39.9 us
    ppermute x9, starting transfers between devices, permute(): return lax.ppermute(value, AXIS, pairs_of(even_step, odd_step))  17.6 us
    ppermute x9, waiting for transfers between devices, permute(): return lax.ppermute(value, AXIS, pairs_of(even_step, odd_step))  11.2 us
  transfers between devices with their start and end apart: 9, of which 3 were waited for; matrix products, arithmetic and copies ran while one was open for 0% of the time, Pallas kernels for 53%

commit v1 on v0

--- a/solution.py
+++ b/solution.py
@@ -15,7 +15,6 @@
 PARTS = 4
 ADD_TILE = 32
 LIMIT = 16 * 1024 * 1024
-W_FINISH = 20e9
 W_CLOSE = 20e9
 W_COPIED = 20e9
 W_ADD = 20e9
@@ -261,23 +260,56 @@
     )
 
 
-def close_kernel(log_scale, bias, labels_x, x, y, before, raw, out):
+def close_kernel(log_scale, bias, labels_x, x, y, before, raw, out, *_):
     for rows, grad in contributions(log_scale, bias, labels_x, x, y):
         out[rows, :] = back_through(raw[rows, :], before[rows, :] + grad)
 
 
 def close(call, scalars, labels_x, x, y, before, raw):
-    args = [*scalars, labels_x, x, y, before, raw]
-    return call(
+    shape = (ROWS, x.shape[1])
+    closed, *outs = call(
         close_kernel,
-        args,
-        [SMEM, SMEM] + [VMEM] * (len(args) - 2),
-        pltpu.VMEM((ROWS, x.shape[1]), jnp.float32),
-        out_specs=VMEM,
+        [*scalars, labels_x, x, y, before, raw],
+        [SMEM, SMEM] + [VMEM] * 5,
+        [pltpu.VMEM(shape, jnp.float32)] + [pltpu.HBM(shape, jnp.float32)] * 2,
+        out_specs=[VMEM, HBM, HBM],
         input_output_aliases={5: 0},
         name="close",
         weight=W_CLOSE,
     )
+    return closed, outs
+
+
+def close_and_store_kernel(
+    log_scale, bias, labels_x, x, y, before, raw, ready, _image_grad, _text_grad, out, image_grad, text_grad, sems
+):
+    image_copies = part_copies(ready, image_grad, sems)
+    text_copies = part_copies(ready, text_grad, sems)
+
+    def start(copies):
+        for copy in copies:
+            copy.start()
+
+    either(is_even(), lambda: start(image_copies), lambda: start(text_copies))
+    close_kernel(log_scale, bias, labels_x, x, y, before, raw, out)
+    for copy in image_copies:
+        copy.wait()
+
+
+def close_and_store(call, scalars, labels_x, x, y, before, raw, ready, outs):
+    shape = (ROWS, x.shape[1])
+    closed, *outs = call(
+        close_and_store_kernel,
+        [*scalars, labels_x, x, y, before, raw, ready, *outs],
+        [SMEM, SMEM] + [VMEM] * 6 + [HBM] * 2,
+        [pltpu.VMEM(shape, jnp.float32)] + [pltpu.HBM(shape, jnp.float32)] * 2,
+        out_specs=[VMEM, HBM, HBM],
+        input_output_aliases={5: 0, 8: 1, 9: 2},
+        scratch_shapes=[pltpu.SemaphoreType.DMA((PARTS,))],
+        name="close",
+        weight=W_CLOSE,
+    )
+    return closed, outs
 
 
 def part_kernel(begin, log_scale, bias, labels_x, x, y, raw, *outs):
@@ -302,40 +334,17 @@
     )
 
 
-def finish_kernel(
-    log_scale, bias, labels_x, x, y, before, raw, closed, image_grad, text_grad, sems
-):
-    copies = []
-    for rows, grad in contributions(log_scale, bias, labels_x, x, y):
-        closed[rows, :] = back_through(raw[rows, :], before[rows, :] + grad)
-        image_copy, text_copy = [
-            pltpu.make_async_copy(closed.at[rows], out.at[rows], sems.at[len(copies)])
-            for out in (image_grad, text_grad)
-        ]
-        either(is_even(), image_copy.start, text_copy.start)
-        copies.append(image_copy)
-    for copy in copies:
-        copy.wait()
-
-
-def finish(call, scalars, labels_x, x, y, before, raw):
-    shape = (ROWS, x.shape[1])
-    _, *outs = call(
-        finish_kernel,
-        [*scalars, labels_x, x, y, before, raw],
-        [SMEM, SMEM] + [VMEM] * 5,
-        [pltpu.VMEM(shape, jnp.float32)] + [pltpu.HBM(shape, jnp.float32)] * 2,
-        out_specs=[VMEM, HBM, HBM],
-        input_output_aliases={5: 0},
-        scratch_shapes=[pltpu.SemaphoreType.DMA((len(tiles_of(ROWS)),))],
-        name="finish",
-        weight=W_FINISH,
-    )
-    return outs
-
-
-def add_kernel(begin, _image_grad, _text_grad, closed, piece, image_grad, text_grad, stage, sems):
-    tiles = [pl.ds(start, ADD_TILE) for start in range(0, piece.shape[0], ADD_TILE)]
+def growing(rows):
+    sizes, start = [], 0
+    while start < rows:
+        size = min(ADD_TILE << len(sizes), rows - start)
+        sizes.append((start, size))
+        start += size
+    return sizes
+
+
+def add_kernel(begin, on, _image_grad, _text_grad, closed, piece, image_grad, text_grad, stage, sems):
+    tiles = [pl.ds(start, size) for start, size in growing(piece.shape[0])]
 
     def work(target):
         copies = []
@@ -349,13 +358,16 @@
         for copy in copies:
             copy.wait()
 
-    either(is_even(), lambda: work(text_grad), lambda: work(image_grad))
-
-
-def add(call, closed, piece, outs, begin):
+    if "even" in on:
+        pl.when(is_even())(lambda: work(text_grad))
+    if "odd" in on:
+        pl.when(jnp.logical_not(is_even()))(lambda: work(image_grad))
+
+
+def add(call, closed, piece, outs, begin, on=("even", "odd")):
     size, width = piece.shape
     return call(
-        functools.partial(add_kernel, begin),
+        functools.partial(add_kernel, begin, on),
         [*outs, closed, piece],
         [HBM, HBM, VMEM, VMEM],
         [pltpu.HBM((ROWS, width), jnp.float32)] * 2,
@@ -363,7 +375,7 @@
         input_output_aliases={0: 0, 1: 1},
         scratch_shapes=[
             pltpu.VMEM((size, width), jnp.float32),
-            pltpu.SemaphoreType.DMA((size // ADD_TILE,)),
+            pltpu.SemaphoreType.DMA((len(growing(size)),)),
         ],
         name="add",
         weight=W_ADD,
@@ -405,13 +417,14 @@
     s1 = swap(x)
     grad_u = score(call, scalars, labels, u, s0, grad_u)
     early, late = part(call, scalars, near_labels, x, s1, x_raw, 0, PIECES)
-    early, late = across(early), across(late)
+    early = across(early)
+    late = across(late)
     grad_v = score(call, scalars, labels, v, x, grad_v)
     grad_u = score(call, scalars, labels, u, s1, grad_u)
 
     s2 = swap(*copied(call, y))
-    outs = finish(call, scalars, labels, u, y, grad_u, u_raw)
-    closed = close(call, scalars, labels, v, s2, grad_v, v_raw)
+    ready, outs = close(call, scalars, labels, u, y, grad_u, u_raw)
+    closed, outs = close_and_store(call, scalars, labels, v, s2, grad_v, v_raw, ready, outs)
     outs = add(call, closed, early, outs, 0)
     return tuple(add(call, closed, late, outs, PIECES[0]))
 

time: 71.1 us -> 71.1 us (level)
  Pallas kernels: 39.9 us -> 38.8 us
  waiting for transfers between devices: 11.2 us -> 12.2 us
    pallas_call x14, Pallas kernels: 39.9 us -> 38.8 us  [__call__(): pl.pallas_call(without_tokens, out_shape=[*out_shape, pltpu.VMEM((8, 128)...]
    ppermute x9, waiting for transfers between devices: 11.2 us -> 12.2 us  [permute(): return lax.ppermute(value, AXIS, pairs_of(even_step, odd_step))]
  transfers between devices with their start and end apart: 9 -> 9, of which waited for: 3 -> 3; matrix products, arithmetic and copies ran while one was open for 0% -> 0% of each run, Pallas kernels for 53% -> 52%
where the time goes in v1:
time: 71.1 us; the launch traced here: 70.9 us
  Pallas kernels  38.8 us (55%)
  starting transfers between devices  17.6 us (25%)
  waiting for transfers between devices  12.2 us (17%)
  between operations  2.27 us (3%)
    pallas_call x14, Pallas kernels, __call__(): pl.pallas_call(without_tokens, out_shape=[*out_shape, pltpu.VMEM((8, 128)...  38.8 us
    ppermute x9, starting transfers between devices, permute(): return lax.ppermute(value, AXIS, pairs_of(even_step, odd_step))  17.6 us
    ppermute x9, waiting for transfers between devices, permute(): return lax.ppermute(value, AXIS, pairs_of(even_step, odd_step))  12.2 us
  transfers between devices with their start and end apart: 9, of which 3 were waited for; matrix products, arithmetic and copies ran while one was open for 0% of the time, Pallas kernels for 52%

profile of v1, /device:TPU:0, one launch (start us, length us, event | category | flops | bytes accessed | tf_op | source)
XLA Modules:
  0.0 70.9 jit_solution(12055439146868930431)
XLA Ops:
  0.6 0.1 collective-permute-start.1
  0.7 8.3 %collective-permute-start.2 = (bf16[768,1152]{1,0:T(8,128)(2,1)}, bf16[768,1152]{1,0:T(8,128)(2,1)S(1)}, u32[]{:S(2)}, u32[]{:S(2)}) collective-permute-start(bf16[768,1152]{1,0:T(8,128)(2,1)} %refs_1_.9), channel_id=1, source_target_pairs={{0,127},{1,0},{2,1},{3,2},{4,3},{5,4},{6,5},{7,6},{8,7},{9,8},{10,... | collective-permute-start | bytes 5308424 | tf_op jit(solution)/shard_map/ppermute | solution.py:391
  10.3 3.4 %own_blocks.1 = (bf16[768,1152]{1,0:T(8,128)(2,1)S(1)}, bf16[768,1152]{1,0:T(8,128)(2,1)S(1)}, bf16[784,1152]{1,0:T(8,128)(2,1)S(1)}, bf16[784,1152]{1,0:T(8,128...) custom-call(bf16[768,1152]{1,0:T(8,128)(2,1)} %refs_0_.9, ...), custom_call_target="tpu_custom_call" | custom-call | flops 20000000000 | tf_op jit(solution)/shard_map/own_blocks/pallas_call | solution.py:56
  13.7 3.4 %score.5 = (f32[768,1152]{1,0:T(8,128)S(1)}, f32[8,128]{1,0:T(8,128)S(1)}) custom-call(f32[1]{0:T(128)S(6)} %copy.29.refs_0_, f32[1]{0:T(128)S(6)} %copy.30.refs_1_, f32[768,1]{1,0:T(8,128)S(1)} %get-tuple-element.44.refs_2_, bf16[784,1152]{1,0:T(8,128)(2,1)S(1)} %get-tuple-element.46.refs_3_.refs_4_.refs_0_, ...), custom_call_target="tpu_custom_call" | custom-call | flops 20000000000 | tf_op jit(solution)/shard_map/score/pallas_call | solution.py:56
  17.1 3.5 %score.6 = (f32[768,1152]{1,0:T(8,128)S(1)}, f32[8,128]{1,0:T(8,128)S(1)}) custom-call(f32[1]{0:T(128)S(6)} %copy.29.refs_0_, f32[1]{0:T(128)S(6)} %copy.30.refs_1_, f32[768,1]{1,0:T(8,128)S(1)} %get-tuple-element.44.refs_2_, bf16[784,1152]{1,0:T(8,128)(2,1)S(1)} %get-tuple-element.45.refs_4_.refs_3_, ...), custom_call_target="tpu_custom_call" | custom-call | flops 20000000000 | tf_op jit(solution)/shard_map/score/pallas_call | solution.py:56
  20.6 0.1 copied.2
  20.7 0.7 collective-permute-start.3
  21.4 0.0 collective-permute-start.5
  21.4 0.0 collective-permute-start
  21.4 8.2 %collective-permute-done.3.refs_2_ = s32[1,768]{1,0:T(1,128)S(1)} collective-permute-done((s32[1,768]{1,0:T(1,128)S(1)}, s32[1,768]{1,0:T(1,128)S(1)}, u32[]{:S(2)}, u32[]{:S(2)}) %collective-permute-start.3) | collective-permute-done | bytes 3104 | tf_op jit(solution)/shard_map/ppermute | solution.py:391
  29.6 0.0 collective-permute-done.1.refs_0_
  29.6 0.0 collective-permute-done.2.refs_1_
  29.6 0.9 %neighbour_block.1 = (bf16[768,1152]{1,0:T(8,128)(2,1)S(1)}, bf16[784,1152]{1,0:T(8,128)(2,1)S(1)}, f32[768,1]{1,0:T(8,128)S(1)}, f32[8,128]{1,0:T(8,128)S(1)}) custom-call(bf16[768,1152]{1,0:T(8,128)(2,1)S(1)} %collective-permute-done.1.refs_0_, bf16[768,1152]{1,0:T(8,128)(2,1)S(1)} %collective-permute-done.2.refs_1_, ...), custom_call_target="tpu_custom_call" | custom-call | flops 20000000000 | tf_op jit(solution)/shard_map/neighbour_block/pallas_call | solution.py:56
  30.5 0.3 collective-permute-start.4
  30.8 0.0 collective-permute-done.5.refs_4_
  30.8 3.6 %score.7 = (f32[768,1152]{1,0:T(8,128)S(1)}, f32[8,128]{1,0:T(8,128)S(1)}) custom-call(f32[1]{0:T(128)S(6)} %copy.29.refs_0_, f32[1]{0:T(128)S(6)} %copy.30.refs_1_, f32[768,1]{1,0:T(8,128)S(1)} %get-tuple-element.44.refs_2_, bf16[784,1152]{1,0:T(8,128)(2,1)S(1)} %get-tuple-element.46.refs_3_.refs_4_.refs_0_, ...), custom_call_target="tpu_custom_call", output_to_operand_aliasing={{0}: (5, {})} | custom-call | flops 20000000000 | tf_op jit(solution)/shard_map/score/pallas_call | solution.py:56
  34.4 0.1 collective-permute-done.4.refs_4_
  34.5 4.3 %part.1 = (bf16[352,1152]{1,0:T(8,128)(2,1)S(1)}, bf16[416,1152]{1,0:T(8,128)(2,1)S(1)}, f32[8,128]{1,0:T(8,128)S(1)}) custom-call(f32[1]{0:T(128)S(6)} %copy.29.refs_0_, f32[1]{0:T(128)S(6)} %copy.30.refs_1_, f32[768,1]{1,0:T(8,128)S(1)} %get-tuple-element.59.refs_2_, bf16[784,1152]{1,0:T(8,128)(2,1)S(1)} %get-tuple-element.54.refs_3_.refs_4_, ...), custom_call_target="tpu_custom_call" | custom-call | flops 20000000000 | tf_op jit(solution)/shard_map/part/pallas_call | solution.py:56
  38.8 7.7 %collective-permute-start.7 = (bf16[352,1152]{1,0:T(8,128)(2,1)S(1)}, bf16[352,1152]{1,0:T(8,128)(2,1)S(1)}, u32[]{:S(2)}, u32[]{:S(2)}) collective-permute-start(bf16[352,1152]{1,0:T(8,128)(2,1)S(1)} %get-tuple-element.78), channel_id=1, source_target_pairs={{0,127},{1,2},{2,1},{3,4},{4,3},{5,6},{6,5},{7,8},{8,7},{9,10},{10... | collective-permute-start | bytes 2433032 | tf_op jit(solution)/shard_map/ppermute | solution.py:391
  46.5 0.3 collective-permute-start.8
  46.8 3.7 %score.8 = (f32[768,1152]{1,0:T(8,128)S(1)}, f32[8,128]{1,0:T(8,128)S(1)}) custom-call(f32[1]{0:T(128)S(6)} %copy.29.refs_0_, f32[1]{0:T(128)S(6)} %copy.30.refs_1_, f32[768,1]{1,0:T(8,128)S(1)} %get-tuple-element.44.refs_2_, bf16[784,1152]{1,0:T(8,128)(2,1)S(1)} %get-tuple-element.45.refs_4_.refs_3_, ...), custom_call_target="tpu_custom_call", output_to_operand_aliasing={{0}: (5, {})} | custom-call | flops 20000000000 | tf_op jit(solution)/shard_map/score/pallas_call | solution.py:56
  50.5 3.7 %score.9 = (f32[768,1152]{1,0:T(8,128)S(1)}, f32[8,128]{1,0:T(8,128)S(1)}) custom-call(f32[1]{0:T(128)S(6)} %copy.29.refs_0_, f32[1]{0:T(128)S(6)} %copy.30.refs_1_, f32[768,1]{1,0:T(8,128)S(1)} %get-tuple-element.44.refs_2_, bf16[784,1152]{1,0:T(8,128)(2,1)S(1)} %get-tuple-element.46.refs_3_.refs_4_.refs_0_, ...), custom_call_target="tpu_custom_call", output_to_operand_aliasing={{0}: (5, {})} | custom-call | flops 20000000000 | tf_op jit(solution)/shard_map/score/pallas_call | solution.py:56
  54.2 0.0 collective-permute-done.refs_0_.refs_4_
  54.3 0.1 copied.3
  54.4 0.3 collective-permute-start.6
  54.7 4.4 %close.2 = (f32[768,1152]{1,0:T(8,128)S(1)}, f32[768,1152]{1,0:T(8,128)}, f32[768,1152]{1,0:T(8,128)}, f32[8,128]{1,0:T(8,128)S(1)}) custom-call(f32[1]{0:T(128)S(6)} %copy.29.refs_0_, f32[1]{0:T(128)S(6)} %copy.30.refs_1_, f32[768,1]{1,0:T(8,128)S(1)} %get-tuple-element.44.refs_2_, ...), custom_call_target="tpu_custom_call", output_to_operand_aliasing={{0}: (5, {})} | custom-call | flops 20000000000 | tf_op jit(solution)/shard_map/close/pallas_call | solution.py:56
  59.1 0.0 collective-permute-done.6.refs_4_
  59.1 4.5 %close.3 = (f32[768,1152]{1,0:T(8,128)S(1)}, f32[768,1152]{1,0:T(8,128)}, f32[768,1152]{1,0:T(8,128)}, f32[8,128]{1,0:T(8,128)S(1)}) custom-call(f32[1]{0:T(128)S(6)} %copy.29.refs_0_, f32[1]{0:T(128)S(6)} %copy.30.refs_1_, f32[768,1]{1,0:T(8,128)S(1)} %get-tuple-element.44.refs_2_, ...), custom_call_target="tpu_custom_call", output_to_operand_aliasing={{0}: (5, {}), {1}: (8, {}), {2}: (9, {})} | custom-call | flops 20000000000 | tf_op jit(solution)/shard_map/close/pallas_call | solution.py:56
  63.7 0.0 collective-permute-done.7.refs_3_
  63.7 1.2 %add.2 = (f32[768,1152]{1,0:T(8,128)}, f32[768,1152]{1,0:T(8,128)}, f32[8,128]{1,0:T(8,128)S(1)}) custom-call(f32[768,1152]{1,0:T(8,128)} %get-tuple-element.75.refs_0_, f32[768,1152]{1,0:T(8,128)} %get-tuple-element.76.refs_1_, f32[768,1152]{1,0:T(8,128)S(1)} %get-tuple-element.77.refs_2_, ...), custom_call_target="tpu_custom_call", output_to_operand_aliasing={{0}: (0, {}), {1}: (1, {})} | custom-call | flops 20000000000 | tf_op jit(solution)/shard_map/add/pallas_call | solution.py:56
  64.9 3.9 %collective-permute-done.8.refs_3_ = bf16[416,1152]{1,0:T(8,128)(2,1)S(1)} collective-permute-done((bf16[416,1152]{1,0:T(8,128)(2,1)S(1)}, bf16[416,1152]{1,0:T(8,128)(2,1)S(1)}, u32[]{:S(2)}, u32[]{:S(2)}) %collective-permute-start.8) | collective-permute-done | bytes 958496 | tf_op jit(solution)/shard_map/ppermute | solution.py:391
  68.8 1.9 %add.3 = (f32[768,1152]{1,0:T(8,128)}, f32[768,1152]{1,0:T(8,128)}, f32[8,128]{1,0:T(8,128)}) custom-call(f32[768,1152]{1,0:T(8,128)} %get-tuple-element.80.refs_0_, f32[768,1152]{1,0:T(8,128)} %get-tuple-element.81.refs_1_, f32[768,1152]{1,0:T(8,128)S(1)} %get-tuple-element.77.refs_2_, ...), custom_call_target="tpu_custom_call", output_to_operand_aliasing={{0}: (0, {}), {1}: (1, {})} | custom-call | flops 20000000000 | tf_op jit(solution)/shard_map/add/pallas_call | solution.py:56
Async XLA Ops:
  0.6 29.0 %collective-permute-start.1 = (bf16[768,1152]{1,0:T(8,128)(2,1)}, bf16[768,1152]{1,0:T(8,128)(2,1)S(1)}, u32[]{:S(2)}, u32[]{:S(2)}) collective-permute-start(bf16[768,1152]{1,0:T(8,128)(2,1)} %refs_0_.9), channel_id=1, source_target_pairs={{0,1},{1,2},{2,3},{3,4},{4,5},{5,6},{6,7},{7,8},{8,9},{9,10},{10,1... | collective-permute-start | bytes 5308424 | tf_op jit(solution)/shard_map/ppermute | solution.py:391
  0.7 28.9 %collective-permute-start.2 = (bf16[768,1152]{1,0:T(8,128)(2,1)}, bf16[768,1152]{1,0:T(8,128)(2,1)S(1)}, u32[]{:S(2)}, u32[]{:S(2)}) collective-permute-start(bf16[768,1152]{1,0:T(8,128)(2,1)} %refs_1_.9), channel_id=1, source_target_pairs={{0,127},{1,0},{2,1},{3,2},{4,3},{5,4},{6,5},{7,6},{8,7},{9,8},{10,... | collective-permute-start | bytes 5308424 | tf_op jit(solution)/shard_map/ppermute | solution.py:391
  20.7 8.9 %collective-permute-start.3 = (s32[1,768]{1,0:T(1,128)S(1)}, s32[1,768]{1,0:T(1,128)S(1)}, u32[]{:S(2)}, u32[]{:S(2)}) collective-permute-start(s32[1,768]{1,0:T(1,128)S(1)} %get-tuple-element.52), channel_id=1, source_target_pairs={{0,127},{1,2},{2,1},{3,4},{4,3},{5,6},{6,5},{7,8},{8,7},{9,10},{10... | collective-permute-start | bytes 9224 | tf_op jit(solution)/shard_map/ppermute | solution.py:391
  21.4 9.4 %collective-permute-start.5 = (bf16[784,1152]{1,0:T(8,128)(2,1)S(1)}, bf16[784,1152]{1,0:T(8,128)(2,1)S(1)}, u32[]{:S(2)}, u32[]{:S(2)}) collective-permute-start(bf16[784,1152]{1,0:T(8,128)(2,1)S(1)} %get-tuple-element.51), channel_id=1, source_target_pairs={{0,1},{1,0},{2,3},{3,2},{4,5},{5,4},{6,7},{7,6},{8,9},{9,8},{10,11... | collective-permute-start | bytes 5419016 | tf_op jit(solution)/shard_map/ppermute | solution.py:391
  21.4 32.8 %collective-permute-start = (bf16[784,1152]{1,0:T(8,128)(2,1)S(1)}, bf16[784,1152]{1,0:T(8,128)(2,1)S(1)}, u32[]{:S(2)}, u32[]{:S(2)}) collective-permute-start(bf16[784,1152]{1,0:T(8,128)(2,1)S(1)} %get-tuple-element.51), channel_id=1, source_target_pairs={{0,3},{1,126},{2,5},{3,0},{4,7},{5,2},{6,9},{7,4},{8,11},{9,6},{10... | collective-permute-start | bytes 5419016 | tf_op jit(solution)/shard_map/ppermute | solution.py:391
  30.5 4.0 %collective-permute-start.4 = (bf16[784,1152]{1,0:T(8,128)(2,1)S(1)}, bf16[784,1152]{1,0:T(8,128)(2,1)S(1)}, u32[]{:S(2)}, u32[]{:S(2)}) collective-permute-start(bf16[784,1152]{1,0:T(8,128)(2,1)S(1)} %get-tuple-element.54.refs_3_.refs_4_), channel_id=1, source_target_pairs={{0,1},{1,0},{2,3},{3,2},{4,5},{5,4},{6,7},{7,6},{8,9},{9,8},{10,11... | collective-permute-start | bytes 5419016 | tf_op jit(solution)/shard_map/ppermute | solution.py:391
  38.8 24.9 %collective-permute-start.7 = (bf16[352,1152]{1,0:T(8,128)(2,1)S(1)}, bf16[352,1152]{1,0:T(8,128)(2,1)S(1)}, u32[]{:S(2)}, u32[]{:S(2)}) collective-permute-start(bf16[352,1152]{1,0:T(8,128)(2,1)S(1)} %get-tuple-element.78), channel_id=1, source_target_pairs={{0,127},{1,2},{2,1},{3,4},{4,3},{5,6},{6,5},{7,8},{8,7},{9,10},{10... | collective-permute-start | bytes 2433032 | tf_op jit(solution)/shard_map/ppermute | solution.py:391
  46.5 22.3 %collective-permute-start.8 = (bf16[416,1152]{1,0:T(8,128)(2,1)S(1)}, bf16[416,1152]{1,0:T(8,128)(2,1)S(1)}, u32[]{:S(2)}, u32[]{:S(2)}) collective-permute-start(bf16[416,1152]{1,0:T(8,128)(2,1)S(1)} %get-tuple-element.82), channel_id=1, source_target_pairs={{0,127},{1,2},{2,1},{3,4},{4,3},{5,6},{6,5},{7,8},{8,7},{9,10},{10... | collective-permute-start | bytes 2875400 | tf_op jit(solution)/shard_map/ppermute | solution.py:391
  54.4 4.7 %collective-permute-start.6 = (bf16[784,1152]{1,0:T(8,128)(2,1)S(1)}, bf16[784,1152]{1,0:T(8,128)(2,1)S(1)}, u32[]{:S(2)}, u32[]{:S(2)}) collective-permute-start(bf16[784,1152]{1,0:T(8,128)(2,1)S(1)} %get-tuple-element.65), channel_id=1, source_target_pairs={{0,1},{1,0},{2,3},{3,2},{4,5},{5,4},{6,7},{7,6},{8,9},{9,8},{10,11... | collective-permute-start | bytes 5419016 | tf_op jit(solution)/shard_map/ppermute | solution.py:391

commit v2 on v1

--- a/solution.py
+++ b/solution.py
@@ -11,9 +11,10 @@
 TILE = 256
 ROWS = 768
 LABEL_ROWS = 16
-PIECES = (352, 416)
+PIECES = (368, 400)
 PARTS = 4
 ADD_TILE = 32
+STRIP = 16
 LIMIT = 16 * 1024 * 1024
 W_CLOSE = 20e9
 W_COPIED = 20e9
@@ -343,31 +344,31 @@
     return sizes
 
 
-def add_kernel(begin, on, _image_grad, _text_grad, closed, piece, image_grad, text_grad, stage, sems):
-    tiles = [pl.ds(start, size) for start, size in growing(piece.shape[0])]
-
-    def work(target):
-        copies = []
-        for rows in tiles:
-            there = pl.ds(begin + rows.start, rows.size)
+def add_kernel(begin, _image_grad, _text_grad, closed, piece, image_grad, text_grad, stage, sems):
+    copies = []
+    for start, size in growing(piece.shape[0]):
+
+        @pl.loop(start // STRIP, (start + size) // STRIP)
+        def _(i):
+            at = pl.multiple_of(i * STRIP, STRIP)
+            rows, there = pl.ds(at, STRIP), pl.ds(pl.multiple_of(begin + at, STRIP), STRIP)
             stage[rows, :] = closed[there, :] + piece[rows, :].astype(jnp.float32)
-            copies.append(
-                pltpu.make_async_copy(stage.at[rows], target.at[there], sems.at[len(copies)])
-            )
-            copies[-1].start()
-        for copy in copies:
-            copy.wait()
-
-    if "even" in on:
-        pl.when(is_even())(lambda: work(text_grad))
-    if "odd" in on:
-        pl.when(jnp.logical_not(is_even()))(lambda: work(image_grad))
-
-
-def add(call, closed, piece, outs, begin, on=("even", "odd")):
+
+        rows, there = pl.ds(start, size), pl.ds(begin + start, size)
+        image_copy, text_copy = [
+            pltpu.make_async_copy(stage.at[rows], out.at[there], sems.at[len(copies)])
+            for out in (image_grad, text_grad)
+        ]
+        either(is_even(), text_copy.start, image_copy.start)
+        copies.append(image_copy)
+    for copy in copies:
+        copy.wait()
+
+
+def add(call, closed, piece, outs, begin):
     size, width = piece.shape
     return call(
-        functools.partial(add_kernel, begin, on),
+        functools.partial(add_kernel, begin),
         [*outs, closed, piece],
         [HBM, HBM, VMEM, VMEM],
         [pltpu.HBM((ROWS, width), jnp.float32)] * 2,

time: 71.1 us -> 71 us (level)
  no operation moved by 1% of the time
where the time goes in v2:
time: 71 us; the launch traced here: 70.9 us
  Pallas kernels  38.8 us (55%)
  starting transfers between devices  17.6 us (25%)
  waiting for transfers between devices  12.2 us (17%)
  between operations  2.27 us (3%)
    pallas_call x14, Pallas kernels, __call__(): pl.pallas_call(without_tokens, out_shape=[*out_shape, pltpu.VMEM((8, 128)...  38.8 us
    ppermute x9, starting transfers between devices, permute(): return lax.ppermute(value, AXIS, pairs_of(even_step, odd_step))  17.6 us
    ppermute x9, waiting for transfers between devices, permute(): return lax.ppermute(value, AXIS, pairs_of(even_step, odd_step))  12.2 us
  transfers between devices with their start and end apart: 9, of which 3 were waited for; matrix products, arithmetic and copies ran while one was open for 0% of the time, Pallas kernels for 52%

profile of v2, /device:TPU:0, one launch (start us, length us, event | category | flops | bytes accessed | tf_op | source)
XLA Modules:
  0.0 70.9 jit_solution(11583418211964813249)
XLA Ops:
  0.6 0.1 collective-permute-start.1
  0.7 8.3 %collective-permute-start.2 = (bf16[768,1152]{1,0:T(8,128)(2,1)}, bf16[768,1152]{1,0:T(8,128)(2,1)S(1)}, u32[]{:S(2)}, u32[]{:S(2)}) collective-permute-start(bf16[768,1152]{1,0:T(8,128)(2,1)} %refs_1_.9), channel_id=1, source_target_pairs={{0,127},{1,0},{2,1},{3,2},{4,3},{5,4},{6,5},{7,6},{8,7},{9,8},{10,... | collective-permute-start | bytes 5308424 | tf_op jit(solution)/shard_map/ppermute | solution.py:392
  10.3 3.4 %own_blocks.1 = (bf16[768,1152]{1,0:T(8,128)(2,1)S(1)}, bf16[768,1152]{1,0:T(8,128)(2,1)S(1)}, bf16[784,1152]{1,0:T(8,128)(2,1)S(1)}, bf16[784,1152]{1,0:T(8,128...) custom-call(bf16[768,1152]{1,0:T(8,128)(2,1)} %refs_0_.9, ...), custom_call_target="tpu_custom_call" | custom-call | flops 20000000000 | tf_op jit(solution)/shard_map/own_blocks/pallas_call | solution.py:57
  13.7 3.4 %score.5 = (f32[768,1152]{1,0:T(8,128)S(1)}, f32[8,128]{1,0:T(8,128)S(1)}) custom-call(f32[1]{0:T(128)S(6)} %copy.29.refs_0_, f32[1]{0:T(128)S(6)} %copy.30.refs_1_, f32[768,1]{1,0:T(8,128)S(1)} %get-tuple-element.44.refs_2_, bf16[784,1152]{1,0:T(8,128)(2,1)S(1)} %get-tuple-element.46.refs_3_.refs_4_.refs_0_, ...), custom_call_target="tpu_custom_call" | custom-call | flops 20000000000 | tf_op jit(solution)/shard_map/score/pallas_call | solution.py:57
  17.1 3.5 %score.6 = (f32[768,1152]{1,0:T(8,128)S(1)}, f32[8,128]{1,0:T(8,128)S(1)}) custom-call(f32[1]{0:T(128)S(6)} %copy.29.refs_0_, f32[1]{0:T(128)S(6)} %copy.30.refs_1_, f32[768,1]{1,0:T(8,128)S(1)} %get-tuple-element.44.refs_2_, bf16[784,1152]{1,0:T(8,128)(2,1)S(1)} %get-tuple-element.45.refs_4_.refs_3_, ...), custom_call_target="tpu_custom_call" | custom-call | flops 20000000000 | tf_op jit(solution)/shard_map/score/pallas_call | solution.py:57
  20.6 0.1 copied.2
  20.8 0.6 collective-permute-start.3
  21.4 0.0 collective-permute-start.5
  21.4 0.0 collective-permute-start
  21.4 8.2 %collective-permute-done.3.refs_2_ = s32[1,768]{1,0:T(1,128)S(1)} collective-permute-done((s32[1,768]{1,0:T(1,128)S(1)}, s32[1,768]{1,0:T(1,128)S(1)}, u32[]{:S(2)}, u32[]{:S(2)}) %collective-permute-start.3) | collective-permute-done | bytes 3104 | tf_op jit(solution)/shard_map/ppermute | solution.py:392
  29.6 0.0 collective-permute-done.1.refs_0_
  29.6 0.0 collective-permute-done.2.refs_1_
  29.6 0.9 %neighbour_block.1 = (bf16[768,1152]{1,0:T(8,128)(2,1)S(1)}, bf16[784,1152]{1,0:T(8,128)(2,1)S(1)}, f32[768,1]{1,0:T(8,128)S(1)}, f32[8,128]{1,0:T(8,128)S(1)}) custom-call(bf16[768,1152]{1,0:T(8,128)(2,1)S(1)} %collective-permute-done.1.refs_0_, bf16[768,1152]{1,0:T(8,128)(2,1)S(1)} %collective-permute-done.2.refs_1_, ...), custom_call_target="tpu_custom_call" | custom-call | flops 20000000000 | tf_op jit(solution)/shard_map/neighbour_block/pallas_call | solution.py:57
  30.5 0.3 collective-permute-start.4
  30.8 0.0 collective-permute-done.5.refs_4_
  30.8 3.6 %score.7 = (f32[768,1152]{1,0:T(8,128)S(1)}, f32[8,128]{1,0:T(8,128)S(1)}) custom-call(f32[1]{0:T(128)S(6)} %copy.29.refs_0_, f32[1]{0:T(128)S(6)} %copy.30.refs_1_, f32[768,1]{1,0:T(8,128)S(1)} %get-tuple-element.44.refs_2_, bf16[784,1152]{1,0:T(8,128)(2,1)S(1)} %get-tuple-element.46.refs_3_.refs_4_.refs_0_, ...), custom_call_target="tpu_custom_call", output_to_operand_aliasing={{0}: (5, {})} | custom-call | flops 20000000000 | tf_op jit(solution)/shard_map/score/pallas_call | solution.py:57
  34.4 0.1 collective-permute-done.4.refs_4_
  34.5 4.3 %part.1 = (bf16[368,1152]{1,0:T(8,128)(2,1)S(1)}, bf16[400,1152]{1,0:T(8,128)(2,1)S(1)}, f32[8,128]{1,0:T(8,128)S(1)}) custom-call(f32[1]{0:T(128)S(6)} %copy.29.refs_0_, f32[1]{0:T(128)S(6)} %copy.30.refs_1_, f32[768,1]{1,0:T(8,128)S(1)} %get-tuple-element.59.refs_2_, bf16[784,1152]{1,0:T(8,128)(2,1)S(1)} %get-tuple-element.54.refs_3_.refs_4_, ...), custom_call_target="tpu_custom_call" | custom-call | flops 20000000000 | tf_op jit(solution)/shard_map/part/pallas_call | solution.py:57
  38.8 7.7 %collective-permute-start.7 = (bf16[368,1152]{1,0:T(8,128)(2,1)S(1)}, bf16[368,1152]{1,0:T(8,128)(2,1)S(1)}, u32[]{:S(2)}, u32[]{:S(2)}) collective-permute-start(bf16[368,1152]{1,0:T(8,128)(2,1)S(1)} %get-tuple-element.78), channel_id=1, source_target_pairs={{0,127},{1,2},{2,1},{3,4},{4,3},{5,6},{6,5},{7,8},{8,7},{9,10},{10... | collective-permute-start | bytes 2543624 | tf_op jit(solution)/shard_map/ppermute | solution.py:392
  46.5 0.3 collective-permute-start.8
  46.8 3.7 %score.8 = (f32[768,1152]{1,0:T(8,128)S(1)}, f32[8,128]{1,0:T(8,128)S(1)}) custom-call(f32[1]{0:T(128)S(6)} %copy.29.refs_0_, f32[1]{0:T(128)S(6)} %copy.30.refs_1_, f32[768,1]{1,0:T(8,128)S(1)} %get-tuple-element.44.refs_2_, bf16[784,1152]{1,0:T(8,128)(2,1)S(1)} %get-tuple-element.45.refs_4_.refs_3_, ...), custom_call_target="tpu_custom_call", output_to_operand_aliasing={{0}: (5, {})} | custom-call | flops 20000000000 | tf_op jit(solution)/shard_map/score/pallas_call | solution.py:57
  50.5 3.7 %score.9 = (f32[768,1152]{1,0:T(8,128)S(1)}, f32[8,128]{1,0:T(8,128)S(1)}) custom-call(f32[1]{0:T(128)S(6)} %copy.29.refs_0_, f32[1]{0:T(128)S(6)} %copy.30.refs_1_, f32[768,1]{1,0:T(8,128)S(1)} %get-tuple-element.44.refs_2_, bf16[784,1152]{1,0:T(8,128)(2,1)S(1)} %get-tuple-element.46.refs_3_.refs_4_.refs_0_, ...), custom_call_target="tpu_custom_call", output_to_operand_aliasing={{0}: (5, {})} | custom-call | flops 20000000000 | tf_op jit(solution)/shard_map/score/pallas_call | solution.py:57
  54.2 0.0 collective-permute-done.refs_0_.refs_4_
  54.2 0.1 copied.3
  54.4 0.3 collective-permute-start.6
  54.7 4.4 %close.2 = (f32[768,1152]{1,0:T(8,128)S(1)}, f32[768,1152]{1,0:T(8,128)}, f32[768,1152]{1,0:T(8,128)}, f32[8,128]{1,0:T(8,128)S(1)}) custom-call(f32[1]{0:T(128)S(6)} %copy.29.refs_0_, f32[1]{0:T(128)S(6)} %copy.30.refs_1_, f32[768,1]{1,0:T(8,128)S(1)} %get-tuple-element.44.refs_2_, ...), custom_call_target="tpu_custom_call", output_to_operand_aliasing={{0}: (5, {})} | custom-call | flops 20000000000 | tf_op jit(solution)/shard_map/close/pallas_call | solution.py:57
  59.1 0.0 collective-permute-done.6.refs_4_
  59.1 4.5 %close.3 = (f32[768,1152]{1,0:T(8,128)S(1)}, f32[768,1152]{1,0:T(8,128)}, f32[768,1152]{1,0:T(8,128)}, f32[8,128]{1,0:T(8,128)S(1)}) custom-call(f32[1]{0:T(128)S(6)} %copy.29.refs_0_, f32[1]{0:T(128)S(6)} %copy.30.refs_1_, f32[768,1]{1,0:T(8,128)S(1)} %get-tuple-element.44.refs_2_, ...), custom_call_target="tpu_custom_call", output_to_operand_aliasing={{0}: (5, {}), {1}: (8, {}), {2}: (9, {})} | custom-call | flops 20000000000 | tf_op jit(solution)/shard_map/close/pallas_call | solution.py:57
  63.7 0.0 collective-permute-done.7.refs_3_
  63.7 1.2 %add.2 = (f32[768,1152]{1,0:T(8,128)}, f32[768,1152]{1,0:T(8,128)}, f32[8,128]{1,0:T(8,128)S(1)}) custom-call(f32[768,1152]{1,0:T(8,128)} %get-tuple-element.75.refs_0_, f32[768,1152]{1,0:T(8,128)} %get-tuple-element.76.refs_1_, f32[768,1152]{1,0:T(8,128)S(1)} %get-tuple-element.77.refs_2_, ...), custom_call_target="tpu_custom_call", output_to_operand_aliasing={{0}: (0, {}), {1}: (1, {})} | custom-call | flops 20000000000 | tf_op jit(solution)/shard_map/add/pallas_call | solution.py:57
  64.9 3.9 %collective-permute-done.8.refs_3_ = bf16[400,1152]{1,0:T(8,128)(2,1)S(1)} collective-permute-done((bf16[400,1152]{1,0:T(8,128)(2,1)S(1)}, bf16[400,1152]{1,0:T(8,128)(2,1)S(1)}, u32[]{:S(2)}, u32[]{:S(2)}) %collective-permute-start.8) | collective-permute-done | bytes 921632 | tf_op jit(solution)/shard_map/ppermute | solution.py:392
  68.8 1.9 %add.3 = (f32[768,1152]{1,0:T(8,128)}, f32[768,1152]{1,0:T(8,128)}, f32[8,128]{1,0:T(8,128)}) custom-call(f32[768,1152]{1,0:T(8,128)} %get-tuple-element.80.refs_0_, f32[768,1152]{1,0:T(8,128)} %get-tuple-element.81.refs_1_, f32[768,1152]{1,0:T(8,128)S(1)} %get-tuple-element.77.refs_2_, ...), custom_call_target="tpu_custom_call", output_to_operand_aliasing={{0}: (0, {}), {1}: (1, {})} | custom-call | flops 20000000000 | tf_op jit(solution)/shard_map/add/pallas_call | solution.py:57
Async XLA Ops:
  0.6 29.0 %collective-permute-start.1 = (bf16[768,1152]{1,0:T(8,128)(2,1)}, bf16[768,1152]{1,0:T(8,128)(2,1)S(1)}, u32[]{:S(2)}, u32[]{:S(2)}) collective-permute-start(bf16[768,1152]{1,0:T(8,128)(2,1)} %refs_0_.9), channel_id=1, source_target_pairs={{0,1},{1,2},{2,3},{3,4},{4,5},{5,6},{6,7},{7,8},{8,9},{9,10},{10,1... | collective-permute-start | bytes 5308424 | tf_op jit(solution)/shard_map/ppermute | solution.py:392
  0.7 28.9 %collective-permute-start.2 = (bf16[768,1152]{1,0:T(8,128)(2,1)}, bf16[768,1152]{1,0:T(8,128)(2,1)S(1)}, u32[]{:S(2)}, u32[]{:S(2)}) collective-permute-start(bf16[768,1152]{1,0:T(8,128)(2,1)} %refs_1_.9), channel_id=1, source_target_pairs={{0,127},{1,0},{2,1},{3,2},{4,3},{5,4},{6,5},{7,6},{8,7},{9,8},{10,... | collective-permute-start | bytes 5308424 | tf_op jit(solution)/shard_map/ppermute | solution.py:392
  20.8 8.8 %collective-permute-start.3 = (s32[1,768]{1,0:T(1,128)S(1)}, s32[1,768]{1,0:T(1,128)S(1)}, u32[]{:S(2)}, u32[]{:S(2)}) collective-permute-start(s32[1,768]{1,0:T(1,128)S(1)} %get-tuple-element.52), channel_id=1, source_target_pairs={{0,127},{1,2},{2,1},{3,4},{4,3},{5,6},{6,5},{7,8},{8,7},{9,10},{10... | collective-permute-start | bytes 9224 | tf_op jit(solution)/shard_map/ppermute | solution.py:392
  21.4 9.4 %collective-permute-start.5 = (bf16[784,1152]{1,0:T(8,128)(2,1)S(1)}, bf16[784,1152]{1,0:T(8,128)(2,1)S(1)}, u32[]{:S(2)}, u32[]{:S(2)}) collective-permute-start(bf16[784,1152]{1,0:T(8,128)(2,1)S(1)} %get-tuple-element.51), channel_id=1, source_target_pairs={{0,1},{1,0},{2,3},{3,2},{4,5},{5,4},{6,7},{7,6},{8,9},{9,8},{10,11... | collective-permute-start | bytes 5419016 | tf_op jit(solution)/shard_map/ppermute | solution.py:392
  21.4 32.8 %collective-permute-start = (bf16[784,1152]{1,0:T(8,128)(2,1)S(1)}, bf16[784,1152]{1,0:T(8,128)(2,1)S(1)}, u32[]{:S(2)}, u32[]{:S(2)}) collective-permute-start(bf16[784,1152]{1,0:T(8,128)(2,1)S(1)} %get-tuple-element.51), channel_id=1, source_target_pairs={{0,3},{1,126},{2,5},{3,0},{4,7},{5,2},{6,9},{7,4},{8,11},{9,6},{10... | collective-permute-start | bytes 5419016 | tf_op jit(solution)/shard_map/ppermute | solution.py:392
  30.5 4.0 %collective-permute-start.4 = (bf16[784,1152]{1,0:T(8,128)(2,1)S(1)}, bf16[784,1152]{1,0:T(8,128)(2,1)S(1)}, u32[]{:S(2)}, u32[]{:S(2)}) collective-permute-start(bf16[784,1152]{1,0:T(8,128)(2,1)S(1)} %get-tuple-element.54.refs_3_.refs_4_), channel_id=1, source_target_pairs={{0,1},{1,0},{2,3},{3,2},{4,5},{5,4},{6,7},{7,6},{8,9},{9,8},{10,11... | collective-permute-start | bytes 5419016 | tf_op jit(solution)/shard_map/ppermute | solution.py:392
  38.8 24.9 %collective-permute-start.7 = (bf16[368,1152]{1,0:T(8,128)(2,1)S(1)}, bf16[368,1152]{1,0:T(8,128)(2,1)S(1)}, u32[]{:S(2)}, u32[]{:S(2)}) collective-permute-start(bf16[368,1152]{1,0:T(8,128)(2,1)S(1)} %get-tuple-element.78), channel_id=1, source_target_pairs={{0,127},{1,2},{2,1},{3,4},{4,3},{5,6},{6,5},{7,8},{8,7},{9,10},{10... | collective-permute-start | bytes 2543624 | tf_op jit(solution)/shard_map/ppermute | solution.py:392
  46.5 22.4 %collective-permute-start.8 = (bf16[400,1152]{1,0:T(8,128)(2,1)S(1)}, bf16[400,1152]{1,0:T(8,128)(2,1)S(1)}, u32[]{:S(2)}, u32[]{:S(2)}) collective-permute-start(bf16[400,1152]{1,0:T(8,128)(2,1)S(1)} %get-tuple-element.82), channel_id=1, source_target_pairs={{0,127},{1,2},{2,1},{3,4},{4,3},{5,6},{6,5},{7,8},{8,7},{9,10},{10... | collective-permute-start | bytes 2764808 | tf_op jit(solution)/shard_map/ppermute | solution.py:392
  54.4 4.7 %collective-permute-start.6 = (bf16[784,1152]{1,0:T(8,128)(2,1)S(1)}, bf16[784,1152]{1,0:T(8,128)(2,1)S(1)}, u32[]{:S(2)}, u32[]{:S(2)}) collective-permute-start(bf16[784,1152]{1,0:T(8,128)(2,1)S(1)} %get-tuple-element.65), channel_id=1, source_target_pairs={{0,1},{1,0},{2,3},{3,2},{4,5},{5,4},{6,7},{7,6},{8,9},{9,8},{10,11... | collective-permute-start | bytes 5419016 | tf_op jit(solution)/shard_map/ppermute | solution.py:392
